TPU v7x, 512 devices: a whole 4x8x8 slice. The times are simulated.
512 devices in a mesh: mesh: 8 (over x, core), fourier: 64 (over z, y).
Axes of the slice: x: 4, y: 8, z: 8, core: 2. Of those that a mesh axis runs over, the one named last changes fastest.
Arguments:
- velocity: bfloat16 [3, 2, 256, 16384], P(None, None, 'fourier', 'mesh'), may hold values from -6 to 6
- vorticity: bfloat16 [3, 2, 256, 16384], P(None, None, 'fourier', 'mesh'), may hold values from -6 to 6
- magnetic: bfloat16 [3, 2, 256, 16384], P(None, None, 'fourier', 'mesh'), may hold values from -6 to 6
- current: bfloat16 [3, 2, 256, 16384], P(None, None, 'fourier', 'mesh'), may hold values from -6 to 6
- rotation: float32 [3], replicated, may hold values from -1 to 1
- fluid_label: int32 [16384], P('mesh'), may hold values from 0 to 1, as said below
- send_rows: int32 [8, 512], P('mesh'), may hold values from 0 to 2047
- recv_rows: int32 [8, 512], P('mesh'), may hold values from 0 to 2047
Outputs:
- nonlinear_modes: bfloat16 [6, 2, 256, 16384], P(None, None, 'fourier', 'mesh')
Inputs may be any that keep to these rules, and one draw needn't show every extreme that they name: `fluid_label`: each block of 2048 nodes has at most 1024 nodes with label 1, and some block has exactly 1024.
All inputs are finite; a program needn't handle non-finite values.
Results may differ from a plain program's by a relative error of at most 0.0071.
Values may be sent and summed in bfloat16 or wider, within the bound.
A program may use at most 64 MiB of HBM per device.

v0:
```python
import math

import jax
import jax.numpy as jnp
from jax import lax
from jax.sharding import PartitionSpec as P


def swapped(array, axis, distance):
    return lax.ppermute(array, axis, [(i, i ^ 1 << distance) for i in range(lax.axis_size(axis))])


def spectral_tables(mode_count, angle_count):
    mode_index = jnp.arange(mode_count, dtype=jnp.int32)
    column = jnp.arange(angle_count, dtype=jnp.int32)
    phase_index = mode_index[:, None] * column[None, :] % angle_count
    angle_grid = phase_index.astype(jnp.float32) * (2.0 * math.pi / angle_count)
    scaling = 1.0 / math.sqrt(angle_count)
    weight = jnp.where(mode_index == 0, 1.0, 2.0).astype(jnp.float32)[:, None]
    forward = jnp.stack([weight * jnp.cos(angle_grid), -weight * jnp.sin(angle_grid)]) * scaling
    inverse = jnp.stack([jnp.cos(angle_grid), -jnp.sin(angle_grid)]) * scaling
    return (forward.astype(jnp.bfloat16), inverse.astype(jnp.bfloat16))


def frame_rotation(rotation, angle_count):
    angle_grid = jnp.arange(angle_count, dtype=jnp.int32).astype(jnp.float32) * (
        2.0 * math.pi / angle_count
    )
    cosine = jnp.cos(angle_grid)
    sine_wave = jnp.sin(angle_grid)
    radial = rotation[0] * cosine + rotation[1] * sine_wave
    azimuthal = -rotation[0] * sine_wave + rotation[1] * cosine
    axial_part = jnp.zeros_like(angle_grid) + rotation[2]
    return jnp.stack([radial, azimuthal, axial_part])[:, None, :]


def cross_product(first_field, second_field):
    return jnp.stack(
        [
            first_field[1] * second_field[2] - first_field[2] * second_field[1],
            first_field[2] * second_field[0] - first_field[0] * second_field[2],
            first_field[0] * second_field[1] - first_field[1] * second_field[0],
        ]
    )


def evaluate(fields, fluid_mask, rotation):
    stacked = jnp.concatenate(fields, axis=0)
    groups = lax.axis_size("fourier")
    comps, parts, mode_local, node_count = stacked.shape
    node_share = node_count // groups
    leaving = stacked.reshape(comps, parts, mode_local, groups, node_share)
    leaving = leaving.transpose(3, 4, 0, 1, 2).reshape(
        groups, node_share * comps * parts * mode_local
    )
    spread = lax.all_to_all(leaving, "fourier", split_axis=0, concat_axis=0, tiled=True)
    mode_count = groups * mode_local
    angle_count = 3 * mode_count
    node_rows = spread.reshape(groups, node_share, comps, parts, mode_local)
    node_rows = node_rows.transpose(1, 2, 3, 0, 4).reshape(node_share * comps, parts * mode_count)
    forward, inverse = spectral_tables(mode_count, angle_count)
    physical = jnp.dot(
        node_rows,
        forward.reshape(parts * mode_count, angle_count),
        preferred_element_type=jnp.float32,
    )
    physical = physical.reshape(node_share, 4, 3, angle_count).transpose(1, 2, 0, 3)
    flow, vortex, bfield, jfield = (physical[0], physical[1], physical[2], physical[3])
    frame_spin = frame_rotation(rotation, angle_count)
    force = (
        cross_product(flow, vortex)
        + cross_product(jfield, bfield)
        - 2.0 * cross_product(frame_spin, flow)
    )
    emotive = cross_product(flow, bfield)
    own_mask = lax.dynamic_slice_in_dim(
        fluid_mask, lax.axis_index("fourier") * node_share, node_share, 0
    )
    products = (jnp.concatenate([force, emotive], axis=0) * own_mask[None, :, None]).astype(
        jnp.bfloat16
    )
    products = products.transpose(1, 0, 2).reshape(node_share * 6, angle_count)
    spectral = lax.dot_general(
        products,
        inverse.reshape(parts * mode_count, angle_count),
        (((1,), (1,)), ((), ())),
        preferred_element_type=jnp.float32,
    )
    returning = spectral.astype(jnp.bfloat16).reshape(node_share, 6, parts, groups, mode_local)
    returning = returning.transpose(3, 0, 1, 2, 4).reshape(
        groups, node_share * 6 * parts * mode_local
    )
    back = lax.all_to_all(returning, "fourier", split_axis=0, concat_axis=0, tiled=True)
    back = back.reshape(groups, node_share, 6, parts, mode_local).transpose(2, 3, 4, 0, 1)
    return back.reshape(6, parts, mode_local, node_count)


def body(velocity, vorticity, magnetic, current, rotation, fluid_label, send_rows, recv_rows):
    fields = (velocity, vorticity, magnetic, current)
    node_count = velocity.shape[3]
    spectral = evaluate(fields, fluid_label.astype(jnp.float32), rotation)
    outgoing = jnp.take(spectral, send_rows[0], axis=3)
    incoming = swapped(outgoing, "mesh", 0)
    lead_shape = incoming.shape[:3]
    shared_count = incoming.shape[3]
    placement_table = (
        recv_rows[0][:, None] == jnp.arange(node_count, dtype=jnp.int32)[None, :]
    ).astype(jnp.bfloat16)
    added = jnp.dot(
        incoming.reshape(-1, shared_count), placement_table, preferred_element_type=jnp.float32
    )
    summed = spectral.astype(jnp.float32) + added.reshape(lead_shape + (node_count,))
    return summed.astype(jnp.bfloat16)


def solution(mesh):
    return jax.shard_map(
        body,
        mesh=mesh,
        in_specs=(
            P(None, None, "fourier", "mesh"),
            P(None, None, "fourier", "mesh"),
            P(None, None, "fourier", "mesh"),
            P(None, None, "fourier", "mesh"),
            P(),
            P("mesh"),
            P("mesh", None),
            P("mesh", None),
        ),
        out_specs=P(None, None, "fourier", "mesh"),
        check_vma=False,
    )
```

profile of v0, /device:TPU:1, one launch (start us, length us, event | category | flops | bytes accessed | tf_op | source)
XLA Modules:
  0.0 103.1 jit_solution(14166176787728106136)
XLA Ops:
  0.0 1.3 %pad_maximum_fusion = bf16[12,2,4,2048]{3,2,1,0:T(4,128)(2,1)S(1)} fusion(bf16[3,2,4,2048]{3,2,1,0:T(4,128)(2,1)} %param.11, bf16[3,2,4,2048]{3,2,1,0:T(4,128)(2,1)} %param.10, bf16[3,2,4,2048]{3,2,1,0:T(4,128)(2,1)} %param.9, bf16[3,2,4,2048]{3,2,1,0:T(4,128)(2,1)} %param.8), kind=kLoop, calls=%fused_computation.26 | loop fusion | flops 589824 | bytes 786432 | tf_op jit(solution)/shard_map/concatenate | solution.py:48
  1.3 0.9 reshape.750
  2.3 0.9 copy.21
  3.7 1.4 %reduce = bf16[64,3072]{0,1:T(8,128)(2,1)S(1)} reduce(bf16[64,1,3072]{0,2,1:T(8,128)(2,1)S(1)} %bitcast.162, bf16[]{:T(256)} %broadcast.365), dimensions={1}, to_apply=%copy.22.reduce_sub_computation | reduce | bytes 786434 | tf_op jit(solution)/shard_map/all_to_all | solution.py:56
  5.3 1.0 reshape.766
  6.4 17.3 %all-to-all-start = ((bf16[64,2,1536]{2,1,0:T(2,128)(2,1)}), bf16[64,2,1536]{2,1,0:T(2,128)(2,1)S(1)}, u32[]{:S(2)}, u32[]{:S(2)}) async-start(bf16[64,2,1536]{2,1,0:T(2,128)(2,1)} %reshape.766), calls=%async_computation | async-start | bytes 786432 | tf_op jit(solution)/shard_map/all_to_all | solution.py:56
  25.0 1.3 %multiply_add_fusion = (f32[768]{0:T(1024)S(1)}, f32[768]{0:T(1024)S(1)}) fusion(f32[]{:T(128)} %bitcast.21, f32[]{:T(128)} %bitcast.22, f32[]{:T(128)S(6)} %neg.22), kind=kLoop, calls=%fused_computation.60 | loop fusion | flops 6144 | bytes 6156 | tf_op jit(solution)/shard_map/add | solution.py:31
  27.1 3.3 %fusion.19 = (f32[1,256,768]{2,1,0:T(8,128)S(1)}, f32[1,256,768]{2,1,0:T(8,128)S(1)}) fusion(f32[256]{0:T(256)S(1)} %fusion.26, f32[256]{0:T(256)S(1)} %compare_select_fusion.2), kind=kLoop, calls=%fused_computation.22 | loop fusion | flops 2162688 | bytes 1574912 | tf_op jit(solution)/shard_map/mul | solution.py:20
  30.5 3.2 %fusion.17 = (f32[1,256,768]{2,1,0:T(8,128)S(1)}, f32[1,256,768]{2,1,0:T(8,128)S(1)}) fusion(), kind=kLoop, calls=%fused_computation.20 | loop fusion | flops 1966080 | bytes 1572864 | tf_op jit(solution)/shard_map/cos | solution.py:20
  33.8 4.7 %all-to-all-done = bf16[64,2,1536]{2,1,0:T(2,128)(2,1)S(1)} async-done(((bf16[64,2,1536]{2,1,0:T(2,128)(2,1)}), bf16[64,2,1536]{2,1,0:T(2,128)(2,1)S(1)}, u32[]{:S(2)}, u32[]{:S(2)}) %all-to-all-start) | async-done | bytes 393248 | tf_op jit(solution)/shard_map/all_to_all | solution.py:56
  38.8 1.8 %copy.23 = bf16[64,1,3072]{0,2,1:T(8,128)(2,1)} copy(bf16[64,1,3072]{2,1,0:T(2,128)(2,1)S(1)} %reshape.767) | data formatting | bytes 786432 | tf_op jit(solution)/shard_map/all_to_all | solution.py:56
  40.7 2.9 %copy.24 = bf16[32,12,2,64,4]{0,4,3,2,1:T(4,128)(2,1)S(1)} copy(bf16[32,12,2,64,4]{3,4,2,1,0:T(4,128)(2,1)} %bitcast.163) | data formatting | bytes 786432 | tf_op jit(solution)/shard_map/transpose | solution.py:60
  46.1 10.2 %reshape.753 = bf16[32,6,2,64,4]{1,0,4,3,2:T(8,128)(2,1)} reshape(bf16[192,512]{0,1:T(8,128)(2,1)S(1)} %copy.27) | data formatting | bytes 393216 | tf_op jit(solution)/shard_map/reshape | solution.py:89
  56.4 6.3 %copy.28 = bf16[64,32,6,2,4]{0,4,3,2,1:T(4,128)(2,1)S(1)} copy(bf16[64,32,6,2,4]{2,1,4,0,3:T(8,128)(2,1)} %bitcast.157) | data formatting | bytes 393216 | tf_op jit(solution)/shard_map/transpose | solution.py:90
  62.7 1.0 reduce.1
  64.6 7.3 %all-to-all-start.1 = ((bf16[64,2,768]{2,1,0:T(2,128)(2,1)}), bf16[64,2,768]{2,1,0:T(2,128)(2,1)S(1)}, u32[]{:S(2)}, u32[]{:S(2)}) async-start(bf16[64,2,768]{2,1,0:T(2,128)(2,1)} %reshape.768), calls=%async_computation.1 | async-start | bytes 393216 | tf_op jit(solution)/shard_map/all_to_all | solution.py:93
  71.9 12.0 %all-to-all-done.1 = bf16[64,2,768]{2,1,0:T(2,128)(2,1)S(1)} async-done(((bf16[64,2,768]{2,1,0:T(2,128)(2,1)}), bf16[64,2,768]{2,1,0:T(2,128)(2,1)S(1)}, u32[]{:S(2)}, u32[]{:S(2)}) %all-to-all-start.1) | async-done | bytes 196640 | tf_op jit(solution)/shard_map/all_to_all | solution.py:93
  85.8 4.8 %copy.33 = bf16[6,2,4,2048]{0,2,3,1:T(4,128)(2,1)} copy(bf16[6,2,4,2048]{3,2,1,0:T(4,128)(2,1)S(1)} %reshape.755) | data formatting | bytes 393216 | tf_op jit(solution)/shard_map/reshape | solution.py:95
  90.6 4.2 %gather_fusion = bf16[512,6,2,4]{1,3,2,0:T(4,128)(2,1)S(1)} fusion(bf16[6,2,4,2048]{0,2,3,1:T(4,128)(2,1)} %copy.33, s32[1024]{0:T(1024)S(1)} %pad_clamp_fusion), kind=kCustom, calls=%fused_computation | custom fusion | bytes 100352 | tf_op jit(solution)/shard_map/jit(_take)/gather | solution.py:102
  94.7 0.9 copy.34
  95.7 4.7 %collective-permute-start = (bf16[6,2,4,512]{3,0,2,1:T(8,128)(2,1)S(1)}, bf16[6,2,4,512]{3,0,2,1:T(8,128)(2,1)S(1)}, u32[]{:S(2)}, u32[]{:S(2)}) collective-permute-start(bf16[6,2,4,512]{3,0,2,1:T(8,128)(2,1)S(1)} %select_bitcast_fusion), channel_id=1, source_target_pairs={{0,64},{64,0},{128,192},{192,128},{256,320},{320,256},{384,448},{4... | collective-permute-start | bytes 147464 | tf_op jit(solution)/shard_map/ppermute | solution.py:10
  100.4 0.9 collective-permute-done
  101.3 1.0 fusion.6
  102.3 0.8 copy.35
  (35 shorter events, 7.9 us)
Async XLA Ops:
  5.1 18.6 %copy-start.1 = (f32[3]{0:T(128)S(1)}, f32[3]{0:T(128)}, u32[]{:S(2)}) copy-start(f32[3]{0:T(128)} %param.12) | copy-start | bytes 40
  6.4 32.2 %all-to-all-start = ((bf16[64,2,1536]{2,1,0:T(2,128)(2,1)}), bf16[64,2,1536]{2,1,0:T(2,128)(2,1)S(1)}, u32[]{:S(2)}, u32[]{:S(2)}) async-start(bf16[64,2,1536]{2,1,0:T(2,128)(2,1)} %reshape.766), calls=%async_computation | async-start | bytes 786432 | tf_op jit(solution)/shard_map/all_to_all | solution.py:56
  62.7 9.2 %copy-start = (s32[1,512]{1,0:T(1,128)S(1)}, s32[1,512]{1,0:T(1,128)}, u32[]{:S(2)}) copy-start(s32[1,512]{1,0:T(1,128)} %param.14) | copy-start | bytes 6148
  64.6 19.4 %all-to-all-start.1 = ((bf16[64,2,768]{2,1,0:T(2,128)(2,1)}), bf16[64,2,768]{2,1,0:T(2,128)(2,1)S(1)}, u32[]{:S(2)}, u32[]{:S(2)}) async-start(bf16[64,2,768]{2,1,0:T(2,128)(2,1)} %reshape.768), calls=%async_computation.1 | async-start | bytes 393216 | tf_op jit(solution)/shard_map/all_to_all | solution.py:93
  85.8 15.5 %copy-start.2 = (s32[1,512]{1,0:T(1,128)S(1)}, s32[1,512]{1,0:T(1,128)}, u32[]{:S(2)}) copy-start(s32[1,512]{1,0:T(1,128)} %param.15) | copy-start | bytes 6148
  95.7 5.6 %collective-permute-start = (bf16[6,2,4,512]{3,0,2,1:T(8,128)(2,1)S(1)}, bf16[6,2,4,512]{3,0,2,1:T(8,128)(2,1)S(1)}, u32[]{:S(2)}, u32[]{:S(2)}) collective-permute-start(bf16[6,2,4,512]{3,0,2,1:T(8,128)(2,1)S(1)} %select_bitcast_fusion), channel_id=1, source_target_pairs={{0,64},{64,0},{128,192},{192,128},{256,320},{320,256},{384,448},{4... | collective-permute-start | bytes 147464 | tf_op jit(solution)/shard_map/ppermute | solution.py:10
where the time goes:
time: 104 us; the launch traced here: 103 us
  local copies, waits for them, and re-layouts  39.8 us (38%)
  starting transfers between devices  29.3 us (28%)
  waiting for transfers between devices  17.6 us (17%)
  other arithmetic  13.4 us (13%)
  matrix products  2.09 us (2%)
    all_to_all x1, starting transfers between devices, evaluate(): lax.all_to_all(leaving, 'fourier', split_axis=0, concat_axis=0, tiled=True)  17.3 us
    all_to_all x1, waiting for transfers between devices, evaluate(): lax.all_to_all(returning, 'fourier', split_axis=0, concat_axis=0, tiled=T...  12 us
    reshape x1, local copies, waits for them, and re-layouts, evaluate(): spectral.astype(jnp.bfloat16)  10.2 us
    all_to_all x1, starting transfers between devices, evaluate(): lax.all_to_all(returning, 'fourier', split_axis=0, concat_axis=0, tiled=T...  7.27 us
    transpose x1, local copies, waits for them, and re-layouts, evaluate(): returning.transpose(3, 0, 1, 2, 4)  6.32 us
    reshape x2, local copies, waits for them, and re-layouts, evaluate(): return back.reshape(6, parts, mode_local, node_count)  5.57 us
    gather x2, local copies, waits for them, and re-layouts, body(): outgoing = jnp.take(spectral, send_rows[0], axis=3)  5.1 us
    all_to_all x1, waiting for transfers between devices, evaluate(): lax.all_to_all(leaving, 'fourier', split_axis=0, concat_axis=0, tiled=True)  4.72 us
  transfers between devices with their start and end apart: 3, of which 3 were waited for; matrix products, arithmetic and copies ran while one was open for 9% of the time, Pallas kernels for 0%

commit v1 on v0

v1 whole, which is shorter than its diff:
```python
import functools
import math

import jax
import jax.numpy as jnp
import ml_dtypes
import numpy as np
from jax import lax
from jax.experimental import pallas as pl
from jax.experimental.pallas import tpu as pltpu
from jax.sharding import PartitionSpec as P

MESH = pl.DeviceIdType.MESH
LANES = 128
VMEM_BYTES = 62 * 1024 * 1024
def spectral_tables(modes, angles, groups):
    index = np.arange(modes, dtype=np.int64)
    phase = (index[:, None] * np.arange(angles)[None, :] % angles).astype(np.float32)
    grid = phase * np.float32(2.0 * math.pi / angles)
    scaling = np.float32(1.0 / math.sqrt(angles))
    weight = np.where(index == 0, 1.0, 2.0).astype(np.float32)[:, None]
    forward = np.stack([weight * np.cos(grid), -weight * np.sin(grid)]) * scaling
    inverse = np.stack([np.cos(grid), -np.sin(grid)]) * scaling

    def by_owner(table):
        table = table.astype(ml_dtypes.bfloat16).reshape(2, groups, modes // groups, angles)
        return table.transpose(1, 0, 2, 3).reshape(2 * modes, angles)

    return np.ascontiguousarray(by_owner(forward).T), by_owner(inverse)


def angle_tables(angles):
    grid = np.arange(angles, dtype=np.float32) * np.float32(2.0 * math.pi / angles)
    wide = lambda a: np.ascontiguousarray(np.broadcast_to(a.astype(np.float32)[:, None], (angles, LANES)))
    both = np.stack([wide(np.cos(grid)), wide(np.sin(grid))])
    both[:, :, LANES // 2 :] = 0.0
    return both


def worker_of(v, parity):
    row = v // 4
    return row * 8 + 2 * lax.rem(v, 4) + lax.rem(row + parity, 2)


def kernel(
    vel, vor, mag, cur, rot, label, send, recv, fwd, inv, trig, out,
    fields, packed, held, phys, prod, spec, own, mine, picked, given,
    fwd_v, inv_v, trig_v, rot_s, label_v, send_v, recv_v, slots, pick, chosen, place, spread,
    load_sem, small_sem, out_sem, held_sem, back_out_sem, own_sem, pair_out_sem, pair_in_sem,
):
    block = lax.axis_index("mesh")
    me = lax.axis_index("fourier")
    groups = lax.axis_size("fourier")
    half = groups // 2
    parity = lax.rem(block, 2)
    partner = block + 1 - 2 * parity
    workers = own.shape[0]
    angles = fwd_v.shape[0]
    nodes = fields.shape[4]
    tiles = nodes // LANES
    shared = send_v.shape[0] * LANES

    tile = (me // 8) * 4 + lax.rem(me, 8) // 2
    is_worker = jnp.logical_and(me < half, worker_of(tile, parity) == me)
    barrier = pltpu.get_barrier_semaphore()

    smalls = [
        pltpu.make_async_copy(label, label_v, small_sem.at[0]),
        pltpu.make_async_copy(send, send_v, small_sem.at[1]),
        pltpu.make_async_copy(recv, recv_v, small_sem.at[2]),
        pltpu.make_async_copy(rot, rot_s, small_sem.at[3]),
    ]
    loads = [
        pltpu.make_async_copy(field, fields.at[f], load_sem.at[3 + f]) for f, field in enumerate((vel, vor, mag, cur))
    ]
    tables = [
        pltpu.make_async_copy(fwd, fwd_v, load_sem.at[0]),
        pltpu.make_async_copy(inv, inv_v, load_sem.at[1]),
        pltpu.make_async_copy(trig, trig_v, load_sem.at[2]),
    ]
    for copy in smalls + loads:
        copy.start()

    @pl.when(is_worker)
    def _():
        def greet(i, _):
            pl.semaphore_signal(
                barrier, inc=1, device_id=(block, lax.rem(me + i, groups)), device_id_type=MESH
            )
            return 0

        lax.fori_loop(1, groups, greet, 0)
        for copy in tables:
            copy.start()

    pl.semaphore_signal(barrier, inc=1, device_id=(partner, me), device_id_type=MESH)

    smalls[0].wait()
    fluid = label_v[...]
    marks = fluid.astype(jnp.bfloat16)
    up_to = lax.broadcasted_iota(jnp.int32, (LANES, LANES), 0) <= lax.broadcasted_iota(jnp.int32, (LANES, LANES), 1)
    before = lax.broadcasted_iota(jnp.int32, (tiles, tiles), 1) < lax.broadcasted_iota(jnp.int32, (tiles, tiles), 0)
    f32 = jnp.float32
    inside = jnp.dot(marks, up_to.astype(f32).astype(jnp.bfloat16), preferred_element_type=f32)
    ahead = jnp.dot(before.astype(f32).astype(jnp.bfloat16), marks, preferred_element_type=f32).astype(jnp.bfloat16)
    ahead = jnp.dot(ahead, jnp.ones((LANES, LANES), jnp.bfloat16), preferred_element_type=f32)
    slot = jnp.where(fluid > 0, (inside + ahead).astype(jnp.int32) - 1, -1)
    slots[...] = slot

    for copy in loads:
        copy.wait()

    @pl.when(is_worker)
    def _():
        pl.semaphore_wait(barrier, workers)

    @pl.when(jnp.logical_not(is_worker))
    def _():
        pl.semaphore_wait(barrier, workers + 1)

    lines = fields.reshape(96, nodes)
    left = lax.broadcasted_iota(jnp.int32, (24, LANES), 1) < LANES // 2
    wide = 2 * LANES
    for q in range(spread.shape[0] // wide):
        total = jnp.zeros((96, wide), f32)
        for t in range(tiles // 2):
            at = slice(t * wide, (t + 1) * wide)
            for i in range(2):
                row = lax.broadcasted_iota(jnp.int32, (wide, LANES), 0) + q * wide
                here = slot[2 * t + i : 2 * t + i + 1, :] == row
                spread[q * wide : (q + 1) * wide, (2 * t + i) * LANES : (2 * t + i + 1) * LANES] = jnp.where(
                    here, 1.0, 0.0
                ).astype(jnp.bfloat16)
            total = total + lax.dot_general(
                lines[:, at], spread[q * wide : (q + 1) * wide, at],
                (((1,), (1,)), ((), ())), preferred_element_type=f32,
            )
        for i in range(2):
            part = total[:, i * LANES : (i + 1) * LANES]
            u, w, b, j = (part[24 * f : 24 * f + 24] for f in range(4))
            turned = [pltpu.roll(x, LANES // 2, 1) for x in (u, w, b, j)]
            first = jnp.concatenate([jnp.where(left, u, turned[3]), jnp.where(left, w, turned[2])])
            second = jnp.concatenate([jnp.where(left, turned[0], j), jnp.where(left, turned[1], b)])
            for k, slab in enumerate((first, second)):
                v = 4 * q + 2 * i + k
                packed[v] = slab.astype(jnp.bfloat16).reshape(6, 2, 4, LANES)
                owner = worker_of(jnp.int32(v), parity)

                @pl.when(owner != me)
                def _():
                    pltpu.make_async_remote_copy(
                        src_ref=packed.at[v], dst_ref=held.at[me],
                        send_sem=out_sem, recv_sem=held_sem.at[me // half],
                        device_id=(block, owner), device_id_type=MESH,
                    ).start()

                @pl.when(owner == me)
                def _():
                    pltpu.make_async_copy(packed.at[v], held.at[me], held_sem.at[me // half]).start()

    for copy in smalls[1:]:
        copy.wait()
    for r in range(shared // LANES):
        wanted = send_v[r : r + 1, :]
        here = jnp.transpose(jnp.broadcast_to(recv_v[r : r + 1, :], (LANES, LANES)))
        for v in range(tiles):
            row = lax.broadcasted_iota(jnp.int32, (LANES, LANES), 0) + v * LANES
            pick[v * LANES : (v + 1) * LANES, r * LANES : (r + 1) * LANES] = jnp.where(
                wanted == row, 1.0, 0.0
            ).astype(jnp.bfloat16)
            col = lax.broadcasted_iota(jnp.int32, (LANES, LANES), 1) + v * LANES
            place[r * LANES : (r + 1) * LANES, v * LANES : (v + 1) * LANES] = jnp.where(
                here == col, 1.0, 0.0
            ).astype(jnp.bfloat16)
    digits = jnp.zeros((8, shared), f32)
    for v in range(tiles):
        code = jnp.broadcast_to(slots[v : v + 1, :], (8, LANES)) + 32
        digit = jnp.where(lax.broadcasted_iota(jnp.int32, (8, LANES), 0) == 0, code >> 5, code & 31)
        digits = digits + jnp.dot(
            digit.astype(f32).astype(jnp.bfloat16), pick[v * LANES : (v + 1) * LANES, :], preferred_element_type=f32
        )
    code = digits.astype(jnp.int32)
    wanted = code[0:1] * 32 + code[1:2] - 32
    for s in range(spread.shape[0] // LANES):
        row = lax.broadcasted_iota(jnp.int32, (LANES, shared), 0) + s * LANES
        chosen[s * LANES : (s + 1) * LANES, :] = jnp.where(wanted == row, 1.0, 0.0).astype(jnp.bfloat16)

    @pl.when(is_worker)
    def _():
        for copy in tables:
            copy.wait()
        turn_x, turn_y, turn_z = rot_s[0] * 2.0, rot_s[1] * 2.0, rot_s[2] * 2.0
        depth = half * 8
        for h in range(2):
            arrived = held.at[pl.ds(0, half)]
            pltpu.make_async_copy(arrived, arrived, held_sem.at[h]).wait()
            for q in range(3):
                both = [
                    held[h * half : (h + 1) * half, 2 * q + i].reshape(depth, LANES) for i in range(2)
                ]
                part = jnp.dot(
                    fwd_v[:, h * depth : (h + 1) * depth],
                    jnp.concatenate(both, axis=1),
                    preferred_element_type=f32,
                )
                if h == 0:
                    phys[q] = part
                else:
                    phys[q] = phys[q] + part

        rows = 16
        near = lax.broadcasted_iota(jnp.int32, (rows, LANES), 1) < LANES // 2
        turn_z = jnp.where(near, turn_z, 0.0)

        def multiply(i, _):
            at = pl.ds(pl.multiple_of(i * rows, rows), rows)
            x = [phys[c // 2, at, (c % 2) * LANES : (c % 2 + 1) * LANES] for c in range(6)]
            cosine, sine = trig_v[0, at, :], trig_v[1, at, :]
            a, d = x[0:3], x[3:6]
            d = [d[0] + (turn_x * cosine + turn_y * sine), d[1] + (turn_y * cosine - turn_x * sine), d[2] + turn_z]
            e = [pltpu.roll(y, LANES // 2, 1) for y in a]
            for c in range(3):
                m, n = (c + 1) % 3, (c + 2) % 3
                force = a[m] * d[n] - a[n] * d[m]
                force = force + pltpu.roll(force, LANES // 2, 1)
                emf = e[m] * d[n] - e[n] * d[m]
                prod[at, c * LANES : (c + 1) * LANES] = jnp.where(near, force, emf).astype(jnp.bfloat16)
            return 0

        lax.fori_loop(0, angles // rows, multiply, 0, unroll=2)

        for h in range(2):
            back = jnp.dot(
                inv_v[h * depth : (h + 1) * depth, :], prod[...], preferred_element_type=f32
            ).astype(jnp.bfloat16)
            for c in range(3):
                spec[h * half : (h + 1) * half, c] = back[:, c * LANES : (c + 1) * LANES].reshape(half, 2, 4, LANES)

            def give(k, _):
                @pl.when(k != me)
                def _():
                    pltpu.make_async_remote_copy(
                        src_ref=spec.at[k], dst_ref=own.at[tile],
                        send_sem=back_out_sem, recv_sem=own_sem,
                        device_id=(block, k), device_id_type=MESH,
                    ).start()

                @pl.when(k == me)
                def _():
                    pltpu.make_async_copy(spec.at[k], own.at[tile], own_sem).start()

                return 0

            lax.fori_loop(h * half, (h + 1) * half, give, 0)

    pltpu.make_async_copy(own, own, own_sem).wait()
    for i in range(workers // 2):
        one, two = (own[2 * i + k].reshape(24, LANES).astype(f32) for k in range(2))
        force = jnp.where(left, one, pltpu.roll(two, LANES // 2, 1))
        emf = jnp.where(left, pltpu.roll(one, LANES // 2, 1), two)
        mine[:, i * LANES : (i + 1) * LANES] = jnp.concatenate([force, emf]).astype(jnp.bfloat16)
    picked[...] = jnp.dot(mine[...], chosen[...], preferred_element_type=f32).astype(jnp.bfloat16)
    swap = pltpu.make_async_remote_copy(
        src_ref=picked, dst_ref=given, send_sem=pair_out_sem, recv_sem=pair_in_sem,
        device_id=(partner, me), device_id_type=MESH,
    )
    swap.start()
    back = jnp.dot(mine[...], spread[...], preferred_element_type=f32)
    swap.wait_recv()
    total = back + jnp.dot(given[...], place[...], preferred_element_type=f32)
    out[...] = total.astype(jnp.bfloat16).reshape(6, 2, 4, nodes)

    swap.wait_send()

    @pl.when(is_worker)
    def _():
        sent = packed.at[pl.ds(0, workers - 1)]
        pltpu.make_async_copy(sent, sent, out_sem).wait()
        gone = spec.at[pl.ds(0, groups - 1)]
        pltpu.make_async_copy(gone, gone, back_out_sem).wait()

    @pl.when(jnp.logical_not(is_worker))
    def _():
        pltpu.make_async_copy(packed, packed, out_sem).wait()


def body(velocity, vorticity, magnetic, current, rotation, fluid_label, send_rows, recv_rows):
    groups = lax.axis_size("fourier")
    comps, parts, local, nodes = velocity.shape
    modes = groups * local
    angles = 3 * modes
    tiles = nodes // LANES
    shared = send_rows.shape[1]
    forward, inverse = spectral_tables(modes, angles, groups)
    trig = angle_tables(angles)
    half16 = jnp.bfloat16
    any_ = pl.BlockSpec(memory_space=pltpu.HBM)
    workers = 16
    fluid_most = nodes // 2
    return pl.pallas_call(
        kernel,
        out_shape=jax.ShapeDtypeStruct((2 * comps, parts, local, nodes), half16),
        in_specs=[any_] * 11,
        out_specs=pl.BlockSpec(memory_space=pltpu.VMEM),
        scratch_shapes=[
            pltpu.VMEM((4, comps, parts, local, nodes), half16),
            pltpu.VMEM((workers, 6, parts, local, LANES), half16),
            pltpu.VMEM((groups, 6, parts, local, LANES), half16),
            pltpu.VMEM((3, angles, 2 * LANES), jnp.float32),
            pltpu.VMEM((angles, 3 * LANES), half16),
            pltpu.VMEM((groups, 3, parts, local, LANES), half16),
            pltpu.VMEM((workers, 3, parts, local, LANES), half16),
            pltpu.VMEM((48, fluid_most), half16),
            pltpu.VMEM((48, shared), half16),
            pltpu.VMEM((48, shared), half16),
            pltpu.VMEM(forward.shape, half16),
            pltpu.VMEM(inverse.shape, half16),
            pltpu.VMEM(trig.shape, jnp.float32),
            pltpu.SMEM((3,), jnp.float32),
            pltpu.VMEM((tiles, LANES), jnp.int32),
            pltpu.VMEM((shared // LANES, LANES), jnp.int32),
            pltpu.VMEM((shared // LANES, LANES), jnp.int32),
            pltpu.VMEM((tiles, LANES), jnp.int32),
            pltpu.VMEM((nodes, shared), half16),
            pltpu.VMEM((fluid_most, shared), half16),
            pltpu.VMEM((shared, nodes), half16),
            pltpu.VMEM((fluid_most, nodes), half16),
            pltpu.SemaphoreType.DMA((7,)),
            pltpu.SemaphoreType.DMA((4,)),
            pltpu.SemaphoreType.DMA,
            pltpu.SemaphoreType.DMA((2,)),
            pltpu.SemaphoreType.DMA,
            pltpu.SemaphoreType.DMA,
            pltpu.SemaphoreType.DMA,
            pltpu.SemaphoreType.DMA,
        ],
        compiler_params=pltpu.CompilerParams(
            collective_id=0, has_side_effects=True, vmem_limit_bytes=VMEM_BYTES
        ),
    )(
        velocity, vorticity, magnetic, current, rotation,
        fluid_label.reshape(tiles, LANES),
        send_rows.reshape(shared // LANES, LANES),
        recv_rows.reshape(shared // LANES, LANES),
        forward, inverse, trig,
    )


def solution(mesh):
    return jax.shard_map(
        body,
        mesh=mesh,
        in_specs=(
            P(None, None, "fourier", "mesh"),
            P(None, None, "fourier", "mesh"),
            P(None, None, "fourier", "mesh"),
            P(None, None, "fourier", "mesh"),
            P(),
            P("mesh"),
            P("mesh", None),
            P("mesh", None),
        ),
        out_specs=P(None, None, "fourier", "mesh"),
        check_vma=False,
    )
```

time: 104 us -> 40.7 us (0.39)
  Pallas kernels: 0 us -> 38.9 us
  local copies, waits for them, and re-layouts: 39.8 us -> 1.69 us
  starting transfers between devices: 29.3 us -> 0 us
  waiting for transfers between devices: 17.6 us -> 0 us
  other arithmetic: 13.4 us -> 0 us
  matrix products: 2.09 us -> 0 us
    pallas_call x0 -> x1, Pallas kernels: none -> 38.9 us  [body(): pl.pallas_call(kernel, out_shape=jax.ShapeDtypeStruct((2 * comps, parts,...]
    all_to_all x2 -> x0, starting transfers between devices: 24.6 us -> none  [the longest x1 17.3 us: evaluate(): lax.all_to_all(leaving, 'fourier', split_axis=0, concat_axis=0, tiled=True)]
    reshape x5 -> x0, local copies, waits for them, and re-layouts: 16.8 us -> none  [the longest x1 10.2 us: evaluate(): spectral.astype(jnp.bfloat16)]
    all_to_all x2 -> x0, waiting for transfers between devices: 16.7 us -> none  [the longest x1 12 us: evaluate(): lax.all_to_all(returning, 'fourier', split_axis=0, concat_axis=0, tiled=T...]
    transpose x5 -> x0, local copies, waits for them, and re-layouts: 10.8 us -> none  [the longest x1 6.32 us: evaluate(): returning.transpose(3, 0, 1, 2, 4)]
    gather x2 -> x0, local copies, waits for them, and re-layouts: 5.1 us -> none  [body(): outgoing = jnp.take(spectral, send_rows[0], axis=3)]
    ppermute x1 -> x0, starting transfers between devices: 4.69 us -> none  [swapped(): lax.ppermute(array, axis, [(i, i ^ 1 << distance) for i in range(lax.axis...]
    mul x1 -> x0, other arithmetic: 3.27 us -> none  [spectral_tables(): -weight * jnp.sin(angle_grid)]
  transfers between devices with their start and end apart: 3 -> 0, of which waited for: 3 -> 0; matrix products, arithmetic and copies ran while one was open for 9% -> 0% of each run, Pallas kernels for 0% -> 0%
where the time goes in v1:
time: 40.7 us; the launch traced here: 40.6 us
  Pallas kernels  38.9 us (96%)
  local copies, waits for them, and re-layouts  1.69 us (4%)
    pallas_call x1, Pallas kernels, body(): pl.pallas_call(kernel, out_shape=jax.ShapeDtypeStruct((2 * comps, parts,...  38.9 us
    unnamed x1, local copies, waits for them, and re-layouts  1.69 us

profile of v1, /device:TPU:1, one launch (start us, length us, event | category | flops | bytes accessed | tf_op | source)
XLA Modules:
  0.0 40.6 jit_solution(17233615494439505331)
XLA Ops:
  0.0 38.9 %shard_map.109 = bf16[6,2,4,2048]{3,2,1,0:T(4,128)(2,1)} custom-call(bf16[3,2,4,2048]{3,2,1,0:T(4,128)(2,1)} %vel.1, bf16[3,2,4,2048]{3,2,1,0:T(4,128)(2,1)} %vor.1, bf16[3,2,4,2048]{3,2,1,0:T(4,128)(2,1)} %mag.1, bf16[3,2,4,2048]{3,2,1,0:T(4,128)(2,1)} %cur.1, f32[3]{0:T(128)} %rot.1, s32[16,128]{1,0:T(8,128)} %bitcast.3, s32[4,128]{1,0:T(4,128)} %bitcast.4, ...), custom_call_target="tpu_custom_call" | custom-call | tf_op jit(solution)/shard_map/pallas_call | solution.py:300
  38.9 1.7 %copy.13 = bf16[6,2,4,2048]{3,2,1,0:T(4,128)(2,1)} copy(bf16[6,2,4,2048]{3,2,1,0:T(4,128)(2,1)} %shard_map.109) | data formatting | bytes 393216

commit v2 on v1

--- a/solution.py
+++ b/solution.py
@@ -13,6 +13,10 @@
 MESH = pl.DeviceIdType.MESH
 LANES = 128
 VMEM_BYTES = 62 * 1024 * 1024
+WORKERS = (
+    (0, 2, 4, 6, 9, 11, 13, 15, 16, 18, 22, 25, 31, 32, 48, 56),
+    (1, 3, 5, 7, 8, 10, 12, 14, 17, 19, 21, 23, 24, 26, 30, 40),
+)
 def spectral_tables(modes, angles, groups):
     index = np.arange(modes, dtype=np.int64)
     phase = (index[:, None] * np.arange(angles)[None, :] % angles).astype(np.float32)
@@ -38,15 +42,14 @@
 
 
 def worker_of(v, parity):
-    row = v // 4
-    return row * 8 + 2 * lax.rem(v, 4) + lax.rem(row + parity, 2)
+    return jnp.where(parity == 0, WORKERS[0][v], WORKERS[1][v])
 
 
 def kernel(
     vel, vor, mag, cur, rot, label, send, recv, fwd, inv, trig, out,
     fields, packed, held, phys, prod, spec, own, mine, picked, given,
-    fwd_v, inv_v, trig_v, rot_s, label_v, send_v, recv_v, slots, pick, chosen, place, spread,
-    load_sem, small_sem, out_sem, held_sem, back_out_sem, own_sem, pair_out_sem, pair_in_sem,
+    fwd_v, inv_v, trig_v, rot_s, label_v, send_v, recv_v, gather, pick, chosen, place, spread,
+    load_sem, small_sem, out_sem, held_sem, back_out_sem, own_sem, pair_out_sem, pair_in_sem, result, done_sem,
 ):
     block = lax.axis_index("mesh")
     me = lax.axis_index("fourier")
@@ -60,8 +63,13 @@
     tiles = nodes // LANES
     shared = send_v.shape[0] * LANES
 
-    tile = (me // 8) * 4 + lax.rem(me, 8) // 2
-    is_worker = jnp.logical_and(me < half, worker_of(tile, parity) == me)
+    tile = jnp.int32(0)
+    works = jnp.int32(0)
+    for v in range(workers):
+        found = worker_of(v, parity) == me
+        tile = tile + jnp.where(found, v, 0)
+        works = works + jnp.where(found, 1, 0)
+    is_worker = works > 0
     barrier = pltpu.get_barrier_semaphore()
 
     smalls = [
@@ -95,17 +103,22 @@
 
     pl.semaphore_signal(barrier, inc=1, device_id=(partner, me), device_id_type=MESH)
 
+    f32 = jnp.float32
+    i16 = jnp.int16
     smalls[0].wait()
     fluid = label_v[...]
     marks = fluid.astype(jnp.bfloat16)
-    up_to = lax.broadcasted_iota(jnp.int32, (LANES, LANES), 0) <= lax.broadcasted_iota(jnp.int32, (LANES, LANES), 1)
+    first = lax.broadcasted_iota(jnp.int32, (LANES, LANES), 0)
+    last = lax.broadcasted_iota(jnp.int32, (LANES, LANES), 1)
+    below = jnp.where(last < first, 2.0, jnp.where(last == first, 1.0, 0.0)).astype(jnp.bfloat16)
     before = lax.broadcasted_iota(jnp.int32, (tiles, tiles), 1) < lax.broadcasted_iota(jnp.int32, (tiles, tiles), 0)
-    f32 = jnp.float32
-    inside = jnp.dot(marks, up_to.astype(f32).astype(jnp.bfloat16), preferred_element_type=f32)
     ahead = jnp.dot(before.astype(f32).astype(jnp.bfloat16), marks, preferred_element_type=f32).astype(jnp.bfloat16)
-    ahead = jnp.dot(ahead, jnp.ones((LANES, LANES), jnp.bfloat16), preferred_element_type=f32)
-    slot = jnp.where(fluid > 0, (inside + ahead).astype(jnp.int32) - 1, -1)
-    slots[...] = slot
+    across = (((1,), (1,)), ((), ()))
+    code = lax.dot_general(below, marks, across, preferred_element_type=f32)
+    code = code + lax.dot_general(
+        jnp.full((LANES, LANES), 2.0, jnp.bfloat16), ahead, across, preferred_element_type=f32
+    )
+    code = code.astype(jnp.int32).astype(i16)
 
     for copy in loads:
         copy.wait()
@@ -121,30 +134,31 @@
     lines = fields.reshape(96, nodes)
     left = lax.broadcasted_iota(jnp.int32, (24, LANES), 1) < LANES // 2
     wide = 2 * LANES
+    one16, zero16 = jnp.ones((LANES, LANES), jnp.bfloat16), jnp.zeros((LANES, LANES), jnp.bfloat16)
     for q in range(spread.shape[0] // wide):
         total = jnp.zeros((96, wide), f32)
-        for t in range(tiles // 2):
+        for t in range(q, tiles // 2):
             at = slice(t * wide, (t + 1) * wide)
-            for i in range(2):
-                row = lax.broadcasted_iota(jnp.int32, (wide, LANES), 0) + q * wide
-                here = slot[2 * t + i : 2 * t + i + 1, :] == row
-                spread[q * wide : (q + 1) * wide, (2 * t + i) * LANES : (2 * t + i + 1) * LANES] = jnp.where(
-                    here, 1.0, 0.0
-                ).astype(jnp.bfloat16)
-            total = total + lax.dot_general(
-                lines[:, at], spread[q * wide : (q + 1) * wide, at],
-                (((1,), (1,)), ((), ())), preferred_element_type=f32,
+            for n in (2 * t, 2 * t + 1):
+                here = jnp.broadcast_to(code[:, n : n + 1], (LANES, LANES))
+                for i in (2 * q, 2 * q + 1):
+                    wanted = (last * 2 + (2 * i * LANES + 1)).astype(i16)
+                    gather[n * LANES : (n + 1) * LANES, i * LANES : (i + 1) * LANES] = jnp.where(
+                        here == wanted, one16, zero16
+                    )
+            total = total + jnp.dot(
+                lines[:, at], gather[at, q * wide : (q + 1) * wide], preferred_element_type=f32
             )
         for i in range(2):
             part = total[:, i * LANES : (i + 1) * LANES]
             u, w, b, j = (part[24 * f : 24 * f + 24] for f in range(4))
             turned = [pltpu.roll(x, LANES // 2, 1) for x in (u, w, b, j)]
-            first = jnp.concatenate([jnp.where(left, u, turned[3]), jnp.where(left, w, turned[2])])
-            second = jnp.concatenate([jnp.where(left, turned[0], j), jnp.where(left, turned[1], b)])
-            for k, slab in enumerate((first, second)):
+            slab_a = jnp.concatenate([jnp.where(left, u, turned[3]), jnp.where(left, w, turned[2])])
+            slab_b = jnp.concatenate([jnp.where(left, turned[0], j), jnp.where(left, turned[1], b)])
+            for k, slab in enumerate((slab_a, slab_b)):
                 v = 4 * q + 2 * i + k
                 packed[v] = slab.astype(jnp.bfloat16).reshape(6, 2, 4, LANES)
-                owner = worker_of(jnp.int32(v), parity)
+                owner = worker_of(v, parity)
 
                 @pl.when(owner != me)
                 def _():
@@ -160,30 +174,37 @@
 
     for copy in smalls[1:]:
         copy.wait()
+    inside = jnp.dot(marks, (first <= last).astype(f32).astype(jnp.bfloat16), preferred_element_type=f32)
+    ahead = jnp.dot(ahead, one16, preferred_element_type=f32)
+    slots = jnp.where(fluid > 0, (inside + ahead).astype(jnp.int32) - 1, -1)
+    for t in range(tiles):
+        here = jnp.broadcast_to(slots[t : t + 1, :], (LANES, LANES)).astype(i16)
+        for i in range(spread.shape[0] // LANES):
+            spread[i * LANES : (i + 1) * LANES, t * LANES : (t + 1) * LANES] = jnp.where(
+                here == (first + i * LANES).astype(i16), one16, zero16
+            )
     for r in range(shared // LANES):
-        wanted = send_v[r : r + 1, :]
-        here = jnp.transpose(jnp.broadcast_to(recv_v[r : r + 1, :], (LANES, LANES)))
+        wanted = jnp.broadcast_to(send_v[r : r + 1, :], (LANES, LANES)).astype(i16)
+        here = jnp.transpose(jnp.broadcast_to(recv_v[r : r + 1, :], (LANES, LANES))).astype(i16)
         for v in range(tiles):
-            row = lax.broadcasted_iota(jnp.int32, (LANES, LANES), 0) + v * LANES
             pick[v * LANES : (v + 1) * LANES, r * LANES : (r + 1) * LANES] = jnp.where(
-                wanted == row, 1.0, 0.0
-            ).astype(jnp.bfloat16)
-            col = lax.broadcasted_iota(jnp.int32, (LANES, LANES), 1) + v * LANES
+                wanted == (first + v * LANES).astype(i16), one16, zero16
+            )
             place[r * LANES : (r + 1) * LANES, v * LANES : (v + 1) * LANES] = jnp.where(
-                here == col, 1.0, 0.0
-            ).astype(jnp.bfloat16)
+                here == (last + v * LANES).astype(i16), one16, zero16
+            )
     digits = jnp.zeros((8, shared), f32)
     for v in range(tiles):
-        code = jnp.broadcast_to(slots[v : v + 1, :], (8, LANES)) + 32
-        digit = jnp.where(lax.broadcasted_iota(jnp.int32, (8, LANES), 0) == 0, code >> 5, code & 31)
+        number = jnp.broadcast_to(slots[v : v + 1, :], (8, LANES)) + 32
+        digit = jnp.where(lax.broadcasted_iota(jnp.int32, (8, LANES), 0) == 0, number >> 5, number & 31)
         digits = digits + jnp.dot(
             digit.astype(f32).astype(jnp.bfloat16), pick[v * LANES : (v + 1) * LANES, :], preferred_element_type=f32
         )
-    code = digits.astype(jnp.int32)
-    wanted = code[0:1] * 32 + code[1:2] - 32
-    for s in range(spread.shape[0] // LANES):
-        row = lax.broadcasted_iota(jnp.int32, (LANES, shared), 0) + s * LANES
-        chosen[s * LANES : (s + 1) * LANES, :] = jnp.where(wanted == row, 1.0, 0.0).astype(jnp.bfloat16)
+    number = digits.astype(jnp.int32)
+    number = number[0:1] * 32 + number[1:2] - 32
+    for i in range(spread.shape[0] // LANES):
+        row = lax.broadcasted_iota(jnp.int32, (LANES, shared), 0) + i * LANES
+        chosen[i * LANES : (i + 1) * LANES, :] = jnp.where(number == row, 1.0, 0.0).astype(jnp.bfloat16)
 
     @pl.when(is_worker)
     def _():
@@ -191,43 +212,39 @@
             copy.wait()
         turn_x, turn_y, turn_z = rot_s[0] * 2.0, rot_s[1] * 2.0, rot_s[2] * 2.0
         depth = half * 8
-        for h in range(2):
-            arrived = held.at[pl.ds(0, half)]
-            pltpu.make_async_copy(arrived, arrived, held_sem.at[h]).wait()
-            for q in range(3):
-                both = [
-                    held[h * half : (h + 1) * half, 2 * q + i].reshape(depth, LANES) for i in range(2)
-                ]
-                part = jnp.dot(
-                    fwd_v[:, h * depth : (h + 1) * depth],
-                    jnp.concatenate(both, axis=1),
-                    preferred_element_type=f32,
-                )
-                if h == 0:
-                    phys[q] = part
-                else:
-                    phys[q] = phys[q] + part
-
         rows = 16
         near = lax.broadcasted_iota(jnp.int32, (rows, LANES), 1) < LANES // 2
         turn_z = jnp.where(near, turn_z, 0.0)
 
-        def multiply(i, _):
-            at = pl.ds(pl.multiple_of(i * rows, rows), rows)
-            x = [phys[c // 2, at, (c % 2) * LANES : (c % 2 + 1) * LANES] for c in range(6)]
-            cosine, sine = trig_v[0, at, :], trig_v[1, at, :]
-            a, d = x[0:3], x[3:6]
-            d = [d[0] + (turn_x * cosine + turn_y * sine), d[1] + (turn_y * cosine - turn_x * sine), d[2] + turn_z]
-            e = [pltpu.roll(y, LANES // 2, 1) for y in a]
-            for c in range(3):
-                m, n = (c + 1) % 3, (c + 2) % 3
-                force = a[m] * d[n] - a[n] * d[m]
-                force = force + pltpu.roll(force, LANES // 2, 1)
-                emf = e[m] * d[n] - e[n] * d[m]
-                prod[at, c * LANES : (c + 1) * LANES] = jnp.where(near, force, emf).astype(jnp.bfloat16)
-            return 0
-
-        lax.fori_loop(0, angles // rows, multiply, 0, unroll=2)
+        def arrived_modes(h):
+            arrived = held.at[pl.ds(0, half)]
+            pltpu.make_async_copy(arrived, arrived, held_sem.at[h]).wait()
+            both = [held[h * half : (h + 1) * half, c].reshape(depth, LANES) for c in range(6)]
+            return [jnp.concatenate(both[2 * q : 2 * q + 2], axis=1) for q in range(3)]
+
+        for q, part in enumerate(arrived_modes(0)):
+            phys[q] = jnp.dot(fwd_v[:, :depth], part, preferred_element_type=f32)
+
+        late = arrived_modes(1)
+        for k in range(3):
+            third = slice(k * (angles // 3), (k + 1) * (angles // 3))
+            for q in range(3):
+                phys[q, third] = phys[q, third] + jnp.dot(
+                    fwd_v[third, depth:], late[q], preferred_element_type=f32
+                )
+            for i in range(angles // 3 // rows):
+                at = slice(third.start + i * rows, third.start + (i + 1) * rows)
+                x = [phys[c // 2, at, (c % 2) * LANES : (c % 2 + 1) * LANES] for c in range(6)]
+                cosine, sine = trig_v[0, at, :], trig_v[1, at, :]
+                a, d = x[0:3], x[3:6]
+                d = [d[0] + (turn_x * cosine + turn_y * sine), d[1] + (turn_y * cosine - turn_x * sine), d[2] + turn_z]
+                e = [pltpu.roll(y, LANES // 2, 1) for y in a]
+                for c in range(3):
+                    m, n = (c + 1) % 3, (c + 2) % 3
+                    force = a[m] * d[n] - a[n] * d[m]
+                    force = force + pltpu.roll(force, LANES // 2, 1)
+                    emf = e[m] * d[n] - e[n] * d[m]
+                    prod[at, c * LANES : (c + 1) * LANES] = jnp.where(near, force, emf).astype(jnp.bfloat16)
 
         for h in range(2):
             back = jnp.dot(
@@ -267,8 +284,16 @@
     swap.start()
     back = jnp.dot(mine[...], spread[...], preferred_element_type=f32)
     swap.wait_recv()
-    total = back + jnp.dot(given[...], place[...], preferred_element_type=f32)
-    out[...] = total.astype(jnp.bfloat16).reshape(6, 2, 4, nodes)
+    step = nodes // 4
+    writes = []
+    for i in range(4):
+        at = slice(i * step, (i + 1) * step)
+        total = back[:, at] + jnp.dot(given[...], place[:, at], preferred_element_type=f32)
+        result[i] = total.astype(jnp.bfloat16).reshape(6, 2, 4, step)
+        writes.append(pltpu.make_async_copy(result.at[i], out.at[:, :, :, pl.ds(i * step, step)], done_sem.at[i]))
+        writes[-1].start()
+    for write in writes:
+        write.wait()
 
     swap.wait_send()
 
@@ -301,7 +326,7 @@
         kernel,
         out_shape=jax.ShapeDtypeStruct((2 * comps, parts, local, nodes), half16),
         in_specs=[any_] * 11,
-        out_specs=pl.BlockSpec(memory_space=pltpu.VMEM),
+        out_specs=pl.BlockSpec(memory_space=pltpu.HBM),
         scratch_shapes=[
             pltpu.VMEM((4, comps, parts, local, nodes), half16),
             pltpu.VMEM((workers, 6, parts, local, LANES), half16),
@@ -320,7 +345,7 @@
             pltpu.VMEM((tiles, LANES), jnp.int32),
             pltpu.VMEM((shared // LANES, LANES), jnp.int32),
             pltpu.VMEM((shared // LANES, LANES), jnp.int32),
-            pltpu.VMEM((tiles, LANES), jnp.int32),
+            pltpu.VMEM((nodes, fluid_most), half16),
             pltpu.VMEM((nodes, shared), half16),
             pltpu.VMEM((fluid_most, shared), half16),
             pltpu.VMEM((shared, nodes), half16),
@@ -333,6 +358,8 @@
             pltpu.SemaphoreType.DMA,
             pltpu.SemaphoreType.DMA,
             pltpu.SemaphoreType.DMA,
+            pltpu.VMEM((4, 2 * comps, parts, local, nodes // 4), half16),
+            pltpu.SemaphoreType.DMA((4,)),
         ],
         compiler_params=pltpu.CompilerParams(
             collective_id=0, has_side_effects=True, vmem_limit_bytes=VMEM_BYTES

time: 40.7 us -> 37.2 us (0.914)
  Pallas kernels: 38.9 us -> 35.3 us
    pallas_call x1, Pallas kernels: 38.9 us -> 35.3 us  [body(): pl.pallas_call(kernel, out_shape=jax.ShapeDtypeStruct((2 * comps, parts,...]
where the time goes in v2:
time: 37.2 us; the launch traced here: 37 us
  Pallas kernels  35.3 us (95%)
  local copies, waits for them, and re-layouts  1.69 us (5%)
    pallas_call x1, Pallas kernels, body(): pl.pallas_call(kernel, out_shape=jax.ShapeDtypeStruct((2 * comps, parts,...  35.3 us
    unnamed x1, local copies, waits for them, and re-layouts  1.69 us

profile of v2, /device:TPU:1, one launch (start us, length us, event | category | flops | bytes accessed | tf_op | source)
XLA Modules:
  0.0 37.0 jit_solution(9723104204789167779)
XLA Ops:
  0.0 35.3 %shard_map.109 = bf16[6,2,4,2048]{3,2,1,0:T(4,128)(2,1)} custom-call(bf16[3,2,4,2048]{3,2,1,0:T(4,128)(2,1)} %vel.1, bf16[3,2,4,2048]{3,2,1,0:T(4,128)(2,1)} %vor.1, bf16[3,2,4,2048]{3,2,1,0:T(4,128)(2,1)} %mag.1, bf16[3,2,4,2048]{3,2,1,0:T(4,128)(2,1)} %cur.1, f32[3]{0:T(128)} %rot.1, s32[16,128]{1,0:T(8,128)} %bitcast.3, s32[4,128]{1,0:T(4,128)} %bitcast.4, ...), custom_call_target="tpu_custom_call" | custom-call | tf_op jit(solution)/shard_map/pallas_call | solution.py:325
  35.3 1.7 %copy.13 = bf16[6,2,4,2048]{3,2,1,0:T(4,128)(2,1)} copy(bf16[6,2,4,2048]{3,2,1,0:T(4,128)(2,1)} %shard_map.109) | data formatting | bytes 393216

commit v3 on v2

--- a/solution.py
+++ b/solution.py
@@ -12,10 +12,10 @@
 
 MESH = pl.DeviceIdType.MESH
 LANES = 128
-VMEM_BYTES = 62 * 1024 * 1024
+VMEM_BYTES = 60 * 1024 * 1024
 WORKERS = (
     (0, 2, 4, 6, 9, 11, 13, 15, 16, 18, 22, 25, 31, 32, 48, 56),
-    (1, 3, 5, 7, 8, 10, 12, 14, 17, 19, 21, 23, 24, 26, 30, 40),
+    (1, 3, 5, 7, 8, 10, 12, 14, 17, 19, 21, 23, 24, 30, 33, 40),
 )
 def spectral_tables(modes, angles, groups):
     index = np.arange(modes, dtype=np.int64)
@@ -36,7 +36,7 @@
 def angle_tables(angles):
     grid = np.arange(angles, dtype=np.float32) * np.float32(2.0 * math.pi / angles)
     wide = lambda a: np.ascontiguousarray(np.broadcast_to(a.astype(np.float32)[:, None], (angles, LANES)))
-    both = np.stack([wide(np.cos(grid)), wide(np.sin(grid))])
+    both = np.stack([wide(np.cos(grid)), wide(np.sin(grid)), np.ones((angles, LANES), np.float32)])
     both[:, :, LANES // 2 :] = 0.0
     return both
 
@@ -49,7 +49,7 @@
     vel, vor, mag, cur, rot, label, send, recv, fwd, inv, trig, out,
     fields, packed, held, phys, prod, spec, own, mine, picked, given,
     fwd_v, inv_v, trig_v, rot_s, label_v, send_v, recv_v, gather, pick, chosen, place, spread,
-    load_sem, small_sem, out_sem, held_sem, back_out_sem, own_sem, pair_out_sem, pair_in_sem, result, done_sem,
+    load_sem, small_sem, out_sem, held_sem, back_out_sem, own_sem, pair_out_sem, pair_in_sem,
 ):
     block = lax.axis_index("mesh")
     me = lax.axis_index("fourier")
@@ -122,14 +122,6 @@
 
     for copy in loads:
         copy.wait()
-
-    @pl.when(is_worker)
-    def _():
-        pl.semaphore_wait(barrier, workers)
-
-    @pl.when(jnp.logical_not(is_worker))
-    def _():
-        pl.semaphore_wait(barrier, workers + 1)
 
     lines = fields.reshape(96, nodes)
     left = lax.broadcasted_iota(jnp.int32, (24, LANES), 1) < LANES // 2
@@ -158,19 +150,31 @@
             for k, slab in enumerate((slab_a, slab_b)):
                 v = 4 * q + 2 * i + k
                 packed[v] = slab.astype(jnp.bfloat16).reshape(6, 2, 4, LANES)
-                owner = worker_of(v, parity)
-
-                @pl.when(owner != me)
-                def _():
-                    pltpu.make_async_remote_copy(
-                        src_ref=packed.at[v], dst_ref=held.at[me],
-                        send_sem=out_sem, recv_sem=held_sem.at[me // half],
-                        device_id=(block, owner), device_id_type=MESH,
-                    ).start()
-
-                @pl.when(owner == me)
-                def _():
-                    pltpu.make_async_copy(packed.at[v], held.at[me], held_sem.at[me // half]).start()
+
+    def leave(v):
+        return pltpu.make_async_remote_copy(
+            src_ref=packed.at[v], dst_ref=held.at[me],
+            send_sem=out_sem, recv_sem=held_sem.at[me // half],
+            device_id=(block, worker_of(v, parity)), device_id_type=MESH,
+        )
+
+    @pl.when(jnp.logical_not(is_worker))
+    def _():
+        pl.semaphore_wait(barrier, workers + 1)
+        for v in range(workers):
+            leave(v).start()
+
+    @pl.when(is_worker)
+    def _():
+        pl.semaphore_wait(barrier, workers)
+        for v in range(workers):
+            @pl.when(worker_of(v, parity) != me)
+            def _():
+                leave(v).start()
+
+            @pl.when(worker_of(v, parity) == me)
+            def _():
+                pltpu.make_async_copy(packed.at[v], held.at[me], held_sem.at[me // half]).start()
 
     for copy in smalls[1:]:
         copy.wait()
@@ -214,7 +218,6 @@
         depth = half * 8
         rows = 16
         near = lax.broadcasted_iota(jnp.int32, (rows, LANES), 1) < LANES // 2
-        turn_z = jnp.where(near, turn_z, 0.0)
 
         def arrived_modes(h):
             arrived = held.at[pl.ds(0, half)]
@@ -222,8 +225,19 @@
             both = [held[h * half : (h + 1) * half, c].reshape(depth, LANES) for c in range(6)]
             return [jnp.concatenate(both[2 * q : 2 * q + 2], axis=1) for q in range(3)]
 
+        cosine, sine = trig_v[0], trig_v[1]
+        spin = [
+            None, None, None,
+            turn_x * cosine + turn_y * sine,
+            turn_y * cosine - turn_x * sine,
+            turn_z * trig_v[2],
+        ]
         for q, part in enumerate(arrived_modes(0)):
-            phys[q] = jnp.dot(fwd_v[:, :depth], part, preferred_element_type=f32)
+            both = jnp.dot(fwd_v[:, :depth], part, preferred_element_type=f32)
+            for i in range(2):
+                lanes = slice(i * LANES, (i + 1) * LANES)
+                turn = spin[2 * q + i]
+                phys[q, :, lanes] = both[:, lanes] if turn is None else both[:, lanes] + turn
 
         late = arrived_modes(1)
         for k in range(3):
@@ -235,9 +249,7 @@
             for i in range(angles // 3 // rows):
                 at = slice(third.start + i * rows, third.start + (i + 1) * rows)
                 x = [phys[c // 2, at, (c % 2) * LANES : (c % 2 + 1) * LANES] for c in range(6)]
-                cosine, sine = trig_v[0, at, :], trig_v[1, at, :]
                 a, d = x[0:3], x[3:6]
-                d = [d[0] + (turn_x * cosine + turn_y * sine), d[1] + (turn_y * cosine - turn_x * sine), d[2] + turn_z]
                 e = [pltpu.roll(y, LANES // 2, 1) for y in a]
                 for c in range(3):
                     m, n = (c + 1) % 3, (c + 2) % 3
@@ -246,12 +258,12 @@
                     emf = e[m] * d[n] - e[n] * d[m]
                     prod[at, c * LANES : (c + 1) * LANES] = jnp.where(near, force, emf).astype(jnp.bfloat16)
 
-        for h in range(2):
+        for begin, end in ((0, groups // 8), (groups // 8, half), (half, groups)):
             back = jnp.dot(
-                inv_v[h * depth : (h + 1) * depth, :], prod[...], preferred_element_type=f32
+                inv_v[begin * 8 : end * 8, :], prod[...], preferred_element_type=f32
             ).astype(jnp.bfloat16)
             for c in range(3):
-                spec[h * half : (h + 1) * half, c] = back[:, c * LANES : (c + 1) * LANES].reshape(half, 2, 4, LANES)
+                spec[begin:end, c] = back[:, c * LANES : (c + 1) * LANES].reshape(end - begin, 2, 4, LANES)
 
             def give(k, _):
                 @pl.when(k != me)
@@ -268,7 +280,7 @@
 
                 return 0
 
-            lax.fori_loop(h * half, (h + 1) * half, give, 0)
+            lax.fori_loop(begin, end, give, 0)
 
     pltpu.make_async_copy(own, own, own_sem).wait()
     for i in range(workers // 2):
@@ -284,16 +296,8 @@
     swap.start()
     back = jnp.dot(mine[...], spread[...], preferred_element_type=f32)
     swap.wait_recv()
-    step = nodes // 4
-    writes = []
-    for i in range(4):
-        at = slice(i * step, (i + 1) * step)
-        total = back[:, at] + jnp.dot(given[...], place[:, at], preferred_element_type=f32)
-        result[i] = total.astype(jnp.bfloat16).reshape(6, 2, 4, step)
-        writes.append(pltpu.make_async_copy(result.at[i], out.at[:, :, :, pl.ds(i * step, step)], done_sem.at[i]))
-        writes[-1].start()
-    for write in writes:
-        write.wait()
+    total = back + jnp.dot(given[...], place[...], preferred_element_type=f32)
+    out[...] = total.astype(jnp.bfloat16).reshape(6, 2, 4, nodes)
 
     swap.wait_send()
 
@@ -324,9 +328,9 @@
     fluid_most = nodes // 2
     return pl.pallas_call(
         kernel,
-        out_shape=jax.ShapeDtypeStruct((2 * comps, parts, local, nodes), half16),
+        out_shape=pltpu.VMEM((2 * comps, parts, local, nodes), half16),
         in_specs=[any_] * 11,
-        out_specs=pl.BlockSpec(memory_space=pltpu.HBM),
+        out_specs=pl.BlockSpec(memory_space=pltpu.VMEM),
         scratch_shapes=[
             pltpu.VMEM((4, comps, parts, local, nodes), half16),
             pltpu.VMEM((workers, 6, parts, local, LANES), half16),
@@ -358,8 +362,6 @@
             pltpu.SemaphoreType.DMA,
             pltpu.SemaphoreType.DMA,
             pltpu.SemaphoreType.DMA,
-            pltpu.VMEM((4, 2 * comps, parts, local, nodes // 4), half16),
-            pltpu.SemaphoreType.DMA((4,)),
         ],
         compiler_params=pltpu.CompilerParams(
             collective_id=0, has_side_effects=True, vmem_limit_bytes=VMEM_BYTES

time: 37.2 us -> 35.2 us (0.946)
  local copies, waits for them, and re-layouts: 1.69 us -> 0.68 us
  Pallas kernels: 35.3 us -> 34.4 us
    unnamed x1, local copies, waits for them, and re-layouts: 1.69 us -> 0.68 us
    pallas_call x1, Pallas kernels: 35.3 us -> 34.4 us  [body(): pl.pallas_call(kernel, out_shape=pltpu.VMEM((2 * comps, parts, local, nod...]
where the time goes in v3:
time: 35.2 us; the launch traced here: 35.1 us
  Pallas kernels  34.4 us (98%)
  local copies, waits for them, and re-layouts  0.68 us (2%)
    pallas_call x1, Pallas kernels, body(): pl.pallas_call(kernel, out_shape=pltpu.VMEM((2 * comps, parts, local, nod...  34.4 us

profile of v3, /device:TPU:1, one launch (start us, length us, event | category | flops | bytes accessed | tf_op | source)
XLA Modules:
  0.0 35.1 jit_solution(5658058739792553693)
XLA Ops:
  0.0 34.4 %shard_map.109 = bf16[6,2,4,2048]{3,2,1,0:T(4,128)(2,1)S(1)} custom-call(bf16[3,2,4,2048]{3,2,1,0:T(4,128)(2,1)} %vel.1, bf16[3,2,4,2048]{3,2,1,0:T(4,128)(2,1)} %vor.1, bf16[3,2,4,2048]{3,2,1,0:T(4,128)(2,1)} %mag.1, bf16[3,2,4,2048]{3,2,1,0:T(4,128)(2,1)} %cur.1, f32[3]{0:T(128)} %rot.1, s32[16,128]{1,0:T(8,128)} %bitcast.3, s32[4,128]{1,0:T(4,128)} %bitcast.4, ...), custom_call_target="tpu_custom_call" | custom-call | tf_op jit(solution)/shard_map/pallas_call | solution.py:329
  34.4 0.7 %copy.13 = bf16[6,2,4,2048]{3,2,1,0:T(4,128)(2,1)} copy(bf16[6,2,4,2048]{3,2,1,0:T(4,128)(2,1)S(1)} %shard_map.109) | data formatting | bytes 393216

commit v4 on v3

--- a/solution.py
+++ b/solution.py
@@ -14,9 +14,10 @@
 LANES = 128
 VMEM_BYTES = 60 * 1024 * 1024
 WORKERS = (
-    (0, 2, 4, 6, 9, 11, 13, 15, 16, 18, 22, 25, 31, 32, 48, 56),
-    (1, 3, 5, 7, 8, 10, 12, 14, 17, 19, 21, 23, 24, 30, 33, 40),
+    (0, 56, 2, 6, 9, 15, 16, 48, 4, 11, 13, 18, 22, 25, 31, 32),
+    (1, 7, 8, 3, 5, 10, 14, 17, 23, 24, 40, 12, 19, 21, 26, 33),
 )
+NEAR = 12
 def spectral_tables(modes, angles, groups):
     index = np.arange(modes, dtype=np.int64)
     phase = (index[:, None] * np.arange(angles)[None, :] % angles).astype(np.float32)
@@ -70,6 +71,7 @@
         tile = tile + jnp.where(found, v, 0)
         works = works + jnp.where(found, 1, 0)
     is_worker = works > 0
+    side = jnp.where(tile < NEAR, 0, 1)
     barrier = pltpu.get_barrier_semaphore()
 
     smalls = [
@@ -270,36 +272,56 @@
                 def _():
                     pltpu.make_async_remote_copy(
                         src_ref=spec.at[k], dst_ref=own.at[tile],
-                        send_sem=back_out_sem, recv_sem=own_sem,
+                        send_sem=back_out_sem, recv_sem=own_sem.at[side],
                         device_id=(block, k), device_id_type=MESH,
                     ).start()
 
                 @pl.when(k == me)
                 def _():
-                    pltpu.make_async_copy(spec.at[k], own.at[tile], own_sem).start()
+                    pltpu.make_async_copy(spec.at[k], own.at[tile], own_sem.at[side]).start()
 
                 return 0
 
             lax.fori_loop(begin, end, give, 0)
 
-    pltpu.make_async_copy(own, own, own_sem).wait()
-    for i in range(workers // 2):
-        one, two = (own[2 * i + k].reshape(24, LANES).astype(f32) for k in range(2))
-        force = jnp.where(left, one, pltpu.roll(two, LANES // 2, 1))
-        emf = jnp.where(left, pltpu.roll(one, LANES // 2, 1), two)
-        mine[:, i * LANES : (i + 1) * LANES] = jnp.concatenate([force, emf]).astype(jnp.bfloat16)
-    picked[...] = jnp.dot(mine[...], chosen[...], preferred_element_type=f32).astype(jnp.bfloat16)
-    swap = pltpu.make_async_remote_copy(
-        src_ref=picked, dst_ref=given, send_sem=pair_out_sem, recv_sem=pair_in_sem,
-        device_id=(partner, me), device_id_type=MESH,
-    )
-    swap.start()
-    back = jnp.dot(mine[...], spread[...], preferred_element_type=f32)
-    swap.wait_recv()
-    total = back + jnp.dot(given[...], place[...], preferred_element_type=f32)
-    out[...] = total.astype(jnp.bfloat16).reshape(6, 2, 4, nodes)
-
-    swap.wait_send()
+    columns = shared // 2
+    chosen_sum = back = None
+    swaps = []
+    for g, (begin, end) in enumerate(((0, NEAR), (NEAR, workers))):
+        come = own.at[pl.ds(begin, end - begin)]
+        pltpu.make_async_copy(come, come, own_sem.at[g]).wait()
+        for i in range(begin // 2, end // 2):
+            one, two = (own[2 * i + k].reshape(24, LANES).astype(f32) for k in range(2))
+            force = jnp.where(left, one, pltpu.roll(two, LANES // 2, 1))
+            emf = jnp.where(left, pltpu.roll(one, LANES // 2, 1), two)
+            mine[:, i * LANES : (i + 1) * LANES] = jnp.concatenate([force, emf]).astype(jnp.bfloat16)
+        at = slice(begin * LANES // 2, end * LANES // 2)
+        if g == 0:
+            chosen_sum = jnp.dot(mine[:, at], chosen[at, :], preferred_element_type=f32)
+            back = jnp.dot(mine[:, at], spread[at, :], preferred_element_type=f32)
+        else:
+            for h in range(2):
+                lanes = slice(h * columns, (h + 1) * columns)
+                part = jnp.dot(mine[:, at], chosen[at, lanes], preferred_element_type=f32)
+                picked[h] = (chosen_sum[:, lanes] + part).astype(jnp.bfloat16)
+                swaps.append(
+                    pltpu.make_async_remote_copy(
+                        src_ref=picked.at[h], dst_ref=given.at[h],
+                        send_sem=pair_out_sem.at[h], recv_sem=pair_in_sem.at[h],
+                        device_id=(partner, me), device_id_type=MESH,
+                    )
+                )
+                swaps[h].start()
+            back = back + jnp.dot(mine[:, at], spread[at, :], preferred_element_type=f32)
+    for h in range(2):
+        swaps[h].wait_recv()
+        back = back + jnp.dot(
+            given[h], place[h * columns : (h + 1) * columns, :], preferred_element_type=f32
+        )
+    out[...] = back.astype(jnp.bfloat16).reshape(6, 2, 4, nodes)
+
+    for swap in swaps:
+        swap.wait_send()
 
     @pl.when(is_worker)
     def _():
@@ -340,8 +362,8 @@
             pltpu.VMEM((groups, 3, parts, local, LANES), half16),
             pltpu.VMEM((workers, 3, parts, local, LANES), half16),
             pltpu.VMEM((48, fluid_most), half16),
-            pltpu.VMEM((48, shared), half16),
-            pltpu.VMEM((48, shared), half16),
+            pltpu.VMEM((2, 48, shared // 2), half16),
+            pltpu.VMEM((2, 48, shared // 2), half16),
             pltpu.VMEM(forward.shape, half16),
             pltpu.VMEM(inverse.shape, half16),
             pltpu.VMEM(trig.shape, jnp.float32),
@@ -359,9 +381,9 @@
             pltpu.SemaphoreType.DMA,
             pltpu.SemaphoreType.DMA((2,)),
             pltpu.SemaphoreType.DMA,
-            pltpu.SemaphoreType.DMA,
-            pltpu.SemaphoreType.DMA,
-            pltpu.SemaphoreType.DMA,
+            pltpu.SemaphoreType.DMA((2,)),
+            pltpu.SemaphoreType.DMA((2,)),
+            pltpu.SemaphoreType.DMA((2,)),
         ],
         compiler_params=pltpu.CompilerParams(
             collective_id=0, has_side_effects=True, vmem_limit_bytes=VMEM_BYTES

time: 35.2 us -> 34.4 us (0.977)
  Pallas kernels: 34.4 us -> 33.6 us
    pallas_call x1, Pallas kernels: 34.4 us -> 33.6 us  [body(): pl.pallas_call(kernel, out_shape=pltpu.VMEM((2 * comps, parts, local, nod...]
where the time goes in v4:
time: 34.4 us; the launch traced here: 34.2 us
  Pallas kernels  33.6 us (98%)
  local copies, waits for them, and re-layouts  0.68 us (2%)
    pallas_call x1, Pallas kernels, body(): pl.pallas_call(kernel, out_shape=pltpu.VMEM((2 * comps, parts, local, nod...  33.6 us

profile of v4, /device:TPU:1, one launch (start us, length us, event | category | flops | bytes accessed | tf_op | source)
XLA Modules:
  0.0 34.2 jit_solution(9571516113540281114)
XLA Ops:
  0.0 33.6 %shard_map.109 = bf16[6,2,4,2048]{3,2,1,0:T(4,128)(2,1)S(1)} custom-call(bf16[3,2,4,2048]{3,2,1,0:T(4,128)(2,1)} %vel.1, bf16[3,2,4,2048]{3,2,1,0:T(4,128)(2,1)} %vor.1, bf16[3,2,4,2048]{3,2,1,0:T(4,128)(2,1)} %mag.1, bf16[3,2,4,2048]{3,2,1,0:T(4,128)(2,1)} %cur.1, f32[3]{0:T(128)} %rot.1, s32[16,128]{1,0:T(8,128)} %bitcast.3, s32[4,128]{1,0:T(4,128)} %bitcast.4, ...), custom_call_target="tpu_custom_call" | custom-call | tf_op jit(solution)/shard_map/pallas_call | solution.py:351
  33.6 0.7 %copy.13 = bf16[6,2,4,2048]{3,2,1,0:T(4,128)(2,1)} copy(bf16[6,2,4,2048]{3,2,1,0:T(4,128)(2,1)S(1)} %shard_map.109) | data formatting | bytes 393216

commit v5 on v4

--- a/solution.py
+++ b/solution.py
@@ -99,7 +99,7 @@
             )
             return 0
 
-        lax.fori_loop(1, groups, greet, 0)
+        lax.fori_loop(1, groups, greet, 0, unroll=9)
         for copy in tables:
             copy.start()
 
@@ -282,7 +282,7 @@
 
                 return 0
 
-            lax.fori_loop(begin, end, give, 0)
+            lax.fori_loop(begin, end, give, 0, unroll=8)
 
     columns = shared // 2
     chosen_sum = back = None

time: 34.4 us -> 34.1 us (level)
  no operation moved by 1% of the time
where the time goes in v5:
time: 34.1 us; the launch traced here: 34 us
  Pallas kernels  33.3 us (98%)
  local copies, waits for them, and re-layouts  0.68 us (2%)
    pallas_call x1, Pallas kernels, body(): pl.pallas_call(kernel, out_shape=pltpu.VMEM((2 * comps, parts, local, nod...  33.3 us

profile of v5, /device:TPU:1, one launch (start us, length us, event | category | flops | bytes accessed | tf_op | source)
XLA Modules:
  0.0 34.0 jit_solution(8157953402625573886)
XLA Ops:
  0.0 33.3 %shard_map.109 = bf16[6,2,4,2048]{3,2,1,0:T(4,128)(2,1)S(1)} custom-call(bf16[3,2,4,2048]{3,2,1,0:T(4,128)(2,1)} %vel.1, bf16[3,2,4,2048]{3,2,1,0:T(4,128)(2,1)} %vor.1, bf16[3,2,4,2048]{3,2,1,0:T(4,128)(2,1)} %mag.1, bf16[3,2,4,2048]{3,2,1,0:T(4,128)(2,1)} %cur.1, f32[3]{0:T(128)} %rot.1, s32[16,128]{1,0:T(8,128)} %bitcast.3, s32[4,128]{1,0:T(4,128)} %bitcast.4, ...), custom_call_target="tpu_custom_call" | custom-call | tf_op jit(solution)/shard_map/pallas_call | solution.py:351
  33.3 0.7 %copy.13 = bf16[6,2,4,2048]{3,2,1,0:T(4,128)(2,1)} copy(bf16[6,2,4,2048]{3,2,1,0:T(4,128)(2,1)S(1)} %shard_map.109) | data formatting | bytes 393216
